TPU v7x, 32 devices: a whole 2x2x4 slice. The times are simulated.
32 devices in a mesh: groups: 2 (over x), row: 16 (over z, y, core).
Axes of the slice: x: 2, y: 2, z: 4, core: 2. Of those that a mesh axis runs over, the one named last changes fastest.
Arguments:
- alignment_embedding: bfloat16 [64, 256, 256], P('groups', 'row'), parts along dimension 0, may hold values from -6 to 6
- standardize_scaling: float32 [256], replicated, may hold values from 0.1 to 1.9
- standardize_offset: float32 [256], replicated, may hold values from -3 to 3
- first_factor_matrix: bfloat16 [256, 32], replicated, may hold values from -0.375 to 0.375
- first_factor_offset: float32 [32], replicated, may hold values from -3 to 3
- second_factor_matrix: bfloat16 [256, 32], replicated, may hold values from -0.375 to 0.375
- second_factor_offset: float32 [32], replicated, may hold values from -3 to 3
- final_matrix: bfloat16 [1024, 128], replicated, may hold values from -1.796875 to 1.796875
- final_offset: float32 [128], replicated, may hold values from -3 to 3
- pairwise_embedding: bfloat16 [512, 256, 128], P(('groups', 'row')), parts along dimension 0, may hold values from -6 to 6
Outputs:
- pair_out: bfloat16 [512, 256, 128], P(('groups', 'row')), parts along dimension 0
There are 2 independent parts, one for each index of `groups`. A program takes and returns all parts, laid end to end along the dimension named above; an argument that names none is the same for every part. Nothing has to cross between parts.
All inputs are finite; a program needn't handle non-finite values.
Results may differ from a plain program's by a relative error of at most 0.0056.
Values may be sent and summed in bfloat16 or wider, within the bound.
A program may use at most 192 MiB of HBM per device.

v0:
```python
import jax
import jax.numpy as jnp
from jax import lax
from jax.sharding import PartitionSpec as P


def standardize_embedding(values, standardize_scaling, standardize_offset):
    x = values.astype(jnp.float32)
    mean = jnp.mean(x, axis=-1, keepdims=True)
    var = jnp.mean((x - mean) * (x - mean), axis=-1, keepdims=True)
    return ((x - mean) * lax.rsqrt(var + 1e-05) * standardize_scaling + standardize_offset).astype(
        jnp.bfloat16
    )


def linear_map(standardized_alignment, coefficient_matrix, offset_vector):
    final_update = jnp.einsum(
        "vot,tw->vow",
        standardized_alignment,
        coefficient_matrix,
        preferred_element_type=jnp.float32,
    )
    return (final_update + offset_vector).astype(jnp.bfloat16)


def pair_update(sequence_rows, cols, final_matrix, final_offset):
    count = sequence_rows.shape[0]
    outer_product = jnp.einsum(
        "kxd,kyr->xydr", sequence_rows, cols, preferred_element_type=jnp.float32
    ) / float(count)
    n_rows = sequence_rows.shape[1]
    n_cols = cols.shape[1]
    outer_product = outer_product.astype(jnp.bfloat16).reshape(n_rows * n_cols, -1)
    update = jnp.dot(outer_product, final_matrix, preferred_element_type=jnp.float32) + final_offset
    return update.reshape(n_rows, n_cols, -1)


def local(
    alignment_embedding,
    standardize_scaling,
    standardize_offset,
    first_factor_matrix,
    first_factor_offset,
    second_factor_matrix,
    second_factor_offset,
    final_matrix,
    final_offset,
    pairwise_embedding,
):
    standardized_alignment = standardize_embedding(
        alignment_embedding, standardize_scaling, standardize_offset
    )
    first_factor = linear_map(standardized_alignment, first_factor_matrix, first_factor_offset)
    cols = linear_map(
        standardize_embedding(
            lax.all_gather(alignment_embedding, "row", axis=1, tiled=True),
            standardize_scaling,
            standardize_offset,
        ),
        second_factor_matrix,
        second_factor_offset,
    )
    update = pair_update(first_factor, cols, final_matrix, final_offset)
    tile = pairwise_embedding.astype(jnp.float32)
    return (tile + update).astype(jnp.bfloat16)


def solution(mesh):
    placed = (
        P("groups", "row", None),
        P(),
        P(),
        P(),
        P(),
        P(),
        P(),
        P(),
        P(),
        P(("groups", "row"), None, None),
    )
    return jax.shard_map(
        local,
        mesh=mesh,
        in_specs=placed,
        out_specs=P(("groups", "row"), None, None),
        check_vma=False,
    )
```

profile of v0, /device:TPU:1, one launch (start us, length us, event | category | flops | bytes accessed | tf_op | source)
XLA Modules:
  0.0 118.3 jit_solution(12773217907143935125)
XLA Ops:
  6.5 0.0 copy-start
  6.5 0.0 all-gather.2.cloned.1.call-start
  6.6 0.7 all-gather.2.cloned.1.call-update
  7.3 1.1 convert_reduce_fusion.1
  8.4 1.2 %fusion.14 = f32[32,16]{1,0:T(8,128)S(1)} fusion(bf16[32,16,256]{2,1,0:T(8,128)(2,1)} %param.10, f32[32,16]{1,0:T(8,128)S(1)} %broadcast_multiply_fusion.1), kind=kLoop, calls=%fused_computation.22 | loop fusion | flops 523776 | bytes 266240 | tf_op jit(solution)/shard_map/reduce_sum | solution.py:10
  9.6 1.2 fusion.17
  10.8 54.5 %all-gather.2.cloned.1.call-done = bf16[32,256,256]{2,1,0:T(8,128)(2,1)} async-done(((bf16[32,16,256]{2,1,0:T(8,128)(2,1)}), bf16[32,256,256]{2,1,0:T(8,128)(2,1)}) %all-gather.2.cloned.1.call-update) | async-done | bytes 4194320 | tf_op jit(solution)/shard_map/all_gather | solution.py:56
  65.3 3.5 %convert_reduce_fusion = f32[32,256]{1,0:T(8,128)S(1)} fusion(bf16[32,256,256]{2,1,0:T(8,128)(2,1)} %all-gather.2.cloned.1.call-done), kind=kLoop, calls=%fused_computation.2 | loop fusion | flops 4186112 | bytes 4227072 | tf_op jit(solution)/shard_map/reduce_sum | solution.py:9
  68.8 0.0 copy-start.3
  68.8 0.0 copy-start.7
  68.8 0.0 copy-start.8
  68.8 4.0 %fusion.2 = f32[32,256]{1,0:T(8,128)S(1)} fusion(bf16[32,256,256]{2,1,0:T(8,128)(2,1)} %all-gather.2.cloned.1.call-done, f32[32,256]{1,0:T(8,128)S(1)} %broadcast_multiply_fusion), kind=kLoop, calls=%fused_computation.5 | loop fusion | flops 8380416 | bytes 4259840 | tf_op jit(solution)/shard_map/reduce_sum | solution.py:10
  72.8 0.0 copy-done.5
  72.8 0.0 copy-done.6
  72.9 0.0 copy-done.9
  72.9 0.0 copy-done.1
  72.9 2.4 %fusion.7 = f32[32,256,32]{1,2,0:T(8,128)S(1)} fusion(bf16[32,256,256]{2,1,0:T(8,128)(2,1)S(1)} %copy-done.1, f32[256]{0:T(256)S(1)} %copy-done.5, f32[256]{0:T(256)S(1)} %copy-done.6, f32[32,256]{1,0:T(8,128)S(1)} %add_rsqrt_fusion, f32[32,256]{1,0:T(8,128)S(1)} %broadcast_multiply_fusion, bf16[256,32]{0,1:T(8,128)(2,1)S(1)} %copy-done.9), kind=kOutput, calls=%fused_computation.11 | convolution fusion | flops 146800640 | bytes 5326848 | tf_op jit(solution)/shard_map/vot,tw->vow/dot_general | solution.py:17
  75.3 0.0 copy-done.3
  75.3 5.4 %fusion.6 = bf16[16,256,32,32]{1,2,0,3:T(8,128)(2,1)} fusion(f32[32,256,32]{1,2,0:T(8,128)S(1)} %fusion.7, f32[32]{0:T(128)S(1)} %copy-done.7, bf16[32,16,256]{2,1,0:T(8,128)(2,1)S(1)} %fusion.17, f32[32]{0:T(128)S(1)} %copy-done.8, bf16[256,32]{0,1:T(8,128)(2,1)S(1)} %copy-done.3), kind=kOutput, calls=%fused_computation.9 | convolution fusion | flops 285769728 | bytes 9715968 | tf_op jit(solution)/shard_map/kxd,kyr->xydr/dot_general | solution.py:28
  80.7 11.4 %copy.11 = bf16[16,256,32,32]{1,0,3,2:T(8,128)(2,1)} copy(bf16[16,256,32,32]{1,2,0,3:T(8,128)(2,1)} %fusion.6) | data formatting | bytes 16777216 | tf_op jit(solution)/shard_map/convert_element_type | solution.py:33
  92.0 12.2 %copy.15 = bf16[128,8,16,256]{3,1,2,0:T(8,128)(2,1)} copy(bf16[128,8,16,256]{3,2,1,0:T(8,128)(2,1)} %bitcast.27) | data formatting | bytes 16777216
  104.3 5.9 %convolution_add_fusion = f32[4096,128]{1,0:T(8,128)S(1)} fusion(bf16[4096,1024]{0,1:T(8,128)(2,1)} %bitcast.26, bf16[1024,128]{1,0:T(8,128)(2,1)S(1)} %copy-done, f32[128]{0:T(128)S(1)} %copy-done.4), kind=kOutput, calls=%fused_computation.10 | convolution fusion | flops 1074266112 | bytes 10748416 | tf_op jit(solution)/shard_map/dot_general | solution.py:34
  110.2 0.0 copy-done.2
  110.2 1.2 %add_convert_fusion = bf16[16,256,128]{2,1,0:T(8,128)(2,1)} fusion(f32[16,256,128]{2,1,0:T(8,128)S(1)} %bitcast.28, bf16[16,256,128]{2,1,0:T(8,128)(2,1)S(1)} %copy-done.2), kind=kLoop, calls=%fused_computation.12 | loop fusion | flops 1572864 | bytes 4194304 | tf_op jit(solution)/shard_map/convert_element_type | solution.py:65
  (14 shorter events, 0.0 us)
Async XLA Ops:
  6.5 97.7 %copy-start = (bf16[1024,128]{1,0:T(8,128)(2,1)S(1)}, bf16[1024,128]{1,0:T(8,128)(2,1)}, u32[]{:S(2)}) copy-start(bf16[1024,128]{1,0:T(8,128)(2,1)} %param.17) | copy-start | bytes 786436
  6.5 66.3 %copy-start.5 = (f32[256]{0:T(256)S(1)}, f32[256]{0:T(256)}, u32[]{:S(2)}) copy-start(f32[256]{0:T(256)} %param.12) | copy-start | bytes 3076
  6.5 66.3 %copy-start.6 = (f32[256]{0:T(256)S(1)}, f32[256]{0:T(256)}, u32[]{:S(2)}) copy-start(f32[256]{0:T(256)} %param.11) | copy-start | bytes 3076
  6.5 66.3 %copy-start.9 = (bf16[256,32]{0,1:T(8,128)(2,1)S(1)}, bf16[256,32]{0,1:T(8,128)(2,1)}, u32[]{:S(2)}) copy-start(bf16[256,32]{0,1:T(8,128)(2,1)} %param.15) | copy-start | bytes 49156
  6.5 58.7 %all-gather.2.cloned.1.call-start = ((), (), s32[]{:S(2)}) async-start(), calls=%async_computation | async-start | bytes 4456448 | tf_op jit(solution)/shard_map/all_gather | solution.py:56
  65.3 7.6 %copy-start.1 = (bf16[32,256,256]{2,1,0:T(8,128)(2,1)S(1)}, bf16[32,256,256]{2,1,0:T(8,128)(2,1)}, u32[]{:S(2)}) copy-start(bf16[32,256,256]{2,1,0:T(8,128)(2,1)} %all-gather.2.cloned.1.call-done) | copy-start | bytes 12582916
  68.8 6.5 %copy-start.3 = (bf16[256,32]{0,1:T(8,128)(2,1)S(1)}, bf16[256,32]{0,1:T(8,128)(2,1)}, u32[]{:S(2)}) copy-start(bf16[256,32]{0,1:T(8,128)(2,1)} %param.13) | copy-start | bytes 49156
  68.8 6.5 %copy-start.7 = (f32[32]{0:T(128)S(1)}, f32[32]{0:T(128)}, u32[]{:S(2)}) copy-start(f32[32]{0:T(128)} %param.16) | copy-start | bytes 388
  68.8 6.5 %copy-start.8 = (f32[32]{0:T(128)S(1)}, f32[32]{0:T(128)}, u32[]{:S(2)}) copy-start(f32[32]{0:T(128)} %param.14) | copy-start | bytes 388
  92.0 12.2 %copy-start.4 = (f32[128]{0:T(128)S(1)}, f32[128]{0:T(128)}, u32[]{:S(2)}) copy-start(f32[128]{0:T(128)} %param.18) | copy-start | bytes 1540
  104.3 5.9 %copy-start.2 = (bf16[16,256,128]{2,1,0:T(8,128)(2,1)S(1)}, bf16[16,256,128]{2,1,0:T(8,128)(2,1)}, u32[]{:S(2)}) copy-start(bf16[16,256,128]{2,1,0:T(8,128)(2,1)} %param.19) | copy-start | bytes 3145732
Sparse Core Ops, SparseCore 0:
  9.5 55.7 all-gather.1
where the time goes:
time: 119 us; the launch traced here: 118 us
  waiting for transfers between devices  55.2 us (46%)
  local copies, waits for them, and re-layouts  23.7 us (20%)
  matrix products  13.6 us (11%)
  between operations  13.6 us (11%)
  other arithmetic  12.2 us (10%)
    all_gather x1, waiting for transfers between devices, local(): lax.all_gather(alignment_embedding, 'row', axis=1, tiled=True)  54.5 us
    unnamed x21, local copies, waits for them, and re-layouts  12.3 us
    convert_element_type x1, local copies, waits for them, and re-layouts, pair_update(): outer_product.astype(jnp.bfloat16).reshape(n_rows * n_cols, -1)  11.4 us
    dot_general x1, matrix products, pair_update(): jnp.dot(outer_product, final_matrix, preferred_element_type=jnp.float32)  5.9 us
    dot_general x1, matrix products, pair_update(): jnp.einsum('kxd,kyr->xydr', sequence_rows, cols, preferred_element_type=j...  5.36 us
    reduce_sum x2, other arithmetic, standardize_embedding(): var = jnp.mean((x - mean) * (x - mean), axis=-1, keepdims=True)  5.17 us
    reduce_sum x2, other arithmetic, standardize_embedding(): mean = jnp.mean(x, axis=-1, keepdims=True)  4.58 us
    dot_general x1, matrix products, linear_map(): jnp.einsum('vot,tw->vow', standardized_alignment, coefficient_matrix, pre...  2.38 us
  transfers between devices with their start and end apart: 1, of which 1 were waited for; matrix products, arithmetic and copies ran while one was open for 3% of the time, Pallas kernels for 0%

commit v1 on v0

v1 whole, which is shorter than its diff:
```python
import functools

import jax
import jax.numpy as jnp
from jax import lax
from jax.experimental import pallas as pl
from jax.experimental.pallas import tpu as pltpu
from jax.sharding import PartitionSpec as P

MESH = pl.DeviceIdType.MESH
LANES = 128


def kernel(
    n_row,
    x_ref,
    scale_ref,
    shift_ref,
    left_w_ref,
    left_b_ref,
    right_w_ref,
    right_b_ref,
    final_hbm,
    final_b_ref,
    pair_hbm,
    out_hbm,
    normed_ref,
    final_ref,
    final32_ref,
    folded_ref,
    turned_ref,
    rows_ref,
    cols_ref,
    pair_ref,
    out_ref,
    pair_sem,
    final_sem,
    out_sem,
    send_sem,
    recv_sem,
):
    depth, res, channels = x_ref.shape
    width = left_w_ref.shape[1]
    cz = final_b_ref.shape[0]
    pack = LANES // depth
    high = width // pack

    me = lax.axis_index("row")
    core = lax.rem(me, 2)
    y = lax.rem(me // 2, 2)
    z = me // 4
    nz = n_row // 4

    def place(z_, y_, core_):
        return z_ * 4 + y_ * 2 + core_

    steps = sorted(range(1, nz), key=lambda d: (min(d, nz - d), d))
    across = place(z, 1 - y, core)
    sibling = place(z, y, 1 - core)
    line = [place(lax.rem(z + d, nz), y, core) for d in steps]

    barrier = pltpu.get_barrier_semaphore()
    for other in line + [across, sibling]:
        pl.semaphore_signal(barrier, inc=1, device_id={"row": other}, device_id_type=MESH)

    pair_copy = pltpu.make_async_copy(pair_hbm, pair_ref, pair_sem)
    final_copy = pltpu.make_async_copy(final_hbm, final_ref, final_sem)
    final_copy.start()
    pair_copy.start()

    x = x_ref[...].astype(jnp.float32).reshape(depth * res, channels)
    mean = jnp.mean(x, axis=-1, keepdims=True)
    centred = x - mean
    var = jnp.mean(centred * centred, axis=-1, keepdims=True)
    normed = centred * lax.rsqrt(var + 1e-05) * scale_ref[...][None, :] + shift_ref[...][None, :]
    for half in range(channels // LANES):
        normed_ref[half] = normed[:, half * LANES : (half + 1) * LANES]

    normed = jnp.concatenate(
        [
            jnp.concatenate(
                [normed_ref[half, pl.ds(j, depth, stride=res), :] for j in range(res)], axis=0
            )
            for half in range(channels // LANES)
        ],
        axis=1,
    ).astype(jnp.bfloat16)

    right = lax.dot_general(
        right_w_ref[...],
        normed,
        (((0,), (1,)), ((), ())),
        preferred_element_type=jnp.float32,
    )
    right = right + right_b_ref[...][:, None]
    right = right.astype(jnp.bfloat16).astype(jnp.float32)
    for block in range(res // pack):
        turned_ref[block] = right[:, block * LANES : (block + 1) * LANES]
    lane_block = lax.broadcasted_iota(jnp.int32, (high, LANES), 1) // depth
    for block in range(res // pack):
        parts = [turned_ref[block, pl.ds(low, high, stride=pack), :] for low in range(pack)]
        for j_low in range(pack):
            value = None
            for low in range(pack):
                moved = parts[low]
                if low != j_low:
                    moved = pltpu.roll(moved, ((low - j_low) % pack) * depth, 1)
                value = moved if value is None else jnp.where(lane_block == low, moved, value)
            j = block * pack + j_low
            rows_ref[pl.ds(j * high, high), :] = value
    cols_ref[me] = jnp.concatenate(
        [rows_ref[pl.ds(h, res, stride=high), :] for h in range(high)], axis=1
    ).astype(jnp.bfloat16)

    pl.semaphore_wait(barrier, nz + 1)
    sends = []

    def send(slot, target):
        copy = pltpu.make_async_remote_copy(
            src_ref=cols_ref.at[slot],
            dst_ref=cols_ref.at[slot],
            send_sem=send_sem.at[len(sends)],
            recv_sem=recv_sem.at[slot],
            device_id={"row": target},
            device_id_type=MESH,
        )
        copy.start()
        sends.append(copy)

    def arrived(slot):
        pltpu.make_async_remote_copy(
            src_ref=cols_ref.at[slot],
            dst_ref=cols_ref.at[slot],
            send_sem=send_sem.at[0],
            recv_sem=recv_sem.at[slot],
            device_id={"row": sibling},
            device_id_type=MESH,
        ).wait_recv()

    for target in line:
        send(me, target)
    send(me, across)
    send(me, sibling)

    left = jnp.dot(normed, left_w_ref[...], preferred_element_type=jnp.float32)
    left = (left + left_b_ref[...][None, :]).astype(jnp.bfloat16)
    final_copy.wait()
    final32_ref[...] = final_ref[...].astype(jnp.float32)

    def fold(e):
        matrix = jnp.concatenate(
            [final32_ref[pl.ds(e + k, width, stride=width), :] for k in range(2)], axis=1
        ).astype(jnp.bfloat16)
        part = jnp.dot(left, matrix, preferred_element_type=jnp.float32) * (1.0 / depth)
        part = part.astype(jnp.bfloat16)
        for k in range(2):
            for i in range(res):
                folded_ref[(e + k) * depth : (e + k + 1) * depth, i * cz : (i + 1) * cz] = part[
                    i * depth : (i + 1) * depth, k * cz : (k + 1) * cz
                ]

    for e in range(0, width // 2, 2):
        fold(e)
    for d in steps:
        slot = place(lax.rem(z + nz - d, nz), y, core)
        arrived(slot)
        send(slot, across)
        send(slot, sibling)
    for e in range(width // 2, width, 2):
        fold(e)
    for d in [0] + steps:
        slot = place(lax.rem(z + nz - d, nz), 1 - y, core)
        arrived(slot)
        send(slot, sibling)
    for y_ in range(2):
        for d in [0] + steps:
            arrived(place(lax.rem(z + nz - d, nz), y_, 1 - core))

    pair_copy.wait()
    cols = cols_ref[...].reshape(n_row * res, width * depth)
    outs = []
    for i in range(0, res, 2):
        update = jnp.dot(
            cols, folded_ref[:, i * cz : (i + 2) * cz], preferred_element_type=jnp.float32
        )
        for k in range(2):
            part = update[:, k * cz : (k + 1) * cz] + final_b_ref[...][None, :]
            out_ref[i + k] = (pair_ref[i + k].astype(jnp.float32) + part).astype(jnp.bfloat16)
        copy = pltpu.make_async_copy(
            out_ref.at[pl.ds(i, 2)], out_hbm.at[pl.ds(i, 2)], out_sem.at[i // 2]
        )
        copy.start()
        outs.append(copy)
    for copy in sends:
        copy.wait_send()
    for copy in outs:
        copy.wait()


def local(n_row, x, scale, shift, left_w, left_b, right_w, right_b, final_w, final_b, pair):
    depth, res, channels = x.shape
    width = left_w.shape[1]
    cz = final_w.shape[1]
    vmem = pl.BlockSpec(memory_space=pltpu.VMEM)
    hbm = pl.BlockSpec(memory_space=pl.ANY)
    return pl.pallas_call(
        functools.partial(kernel, n_row),
        out_shape=jax.ShapeDtypeStruct(pair.shape, pair.dtype),
        in_specs=[vmem] * 7 + [hbm, vmem, hbm],
        out_specs=hbm,
        scratch_shapes=[
            pltpu.VMEM((channels // LANES, depth * res, LANES), jnp.float32),
            pltpu.VMEM(final_w.shape, jnp.bfloat16),
            pltpu.VMEM(final_w.shape, jnp.float32),
            pltpu.VMEM((width * depth, res * cz), jnp.bfloat16),
            pltpu.VMEM((res * depth // LANES, width, LANES), jnp.float32),
            pltpu.VMEM((res * width * depth // LANES, LANES), jnp.float32),
            pltpu.VMEM((n_row, res, width * depth), jnp.bfloat16),
            pltpu.VMEM(pair.shape, jnp.bfloat16),
            pltpu.VMEM(pair.shape, jnp.bfloat16),
            pltpu.SemaphoreType.DMA,
            pltpu.SemaphoreType.DMA,
            pltpu.SemaphoreType.DMA((res // 2,)),
            pltpu.SemaphoreType.DMA((n_row - 1,)),
            pltpu.SemaphoreType.DMA((n_row,)),
        ],
        compiler_params=pltpu.CompilerParams(
            collective_id=0, has_side_effects=True, vmem_limit_bytes=48 * 1024 * 1024
        ),
    )(x, scale, shift, left_w, left_b, right_w, right_b, final_w, final_b, pair)


def solution(mesh):
    placed = (
        P("groups", "row", None),
        P(),
        P(),
        P(),
        P(),
        P(),
        P(),
        P(),
        P(),
        P(("groups", "row"), None, None),
    )
    return jax.shard_map(
        functools.partial(local, mesh.shape["row"]),
        mesh=mesh,
        in_specs=placed,
        out_specs=P(("groups", "row"), None, None),
        check_vma=False,
    )
```

time: 119 us -> 24.4 us (0.21)
  waiting for transfers between devices: 55.2 us -> 0 us
  Pallas kernels: 0 us -> 18.4 us
  local copies, waits for them, and re-layouts: 23.7 us -> 5.63 us
  matrix products: 13.6 us -> 0 us
  between operations: 13.6 us -> 0.06 us
  other arithmetic: 12.2 us -> 0 us
    all_gather x1 -> x0, waiting for transfers between devices: 54.5 us -> none  [local(): lax.all_gather(alignment_embedding, 'row', axis=1, tiled=True)]
    pallas_call x0 -> x1, Pallas kernels: none -> 18.4 us  [local(): pl.pallas_call(functools.partial(kernel, n_row), out_shape=jax.ShapeDtype...]
    dot_general x3 -> x0, matrix products: 13.6 us -> none  [the longest x1 5.9 us: pair_update(): jnp.dot(outer_product, final_matrix, preferred_element_type=jnp.float32)]
    convert_element_type x1 -> x0, local copies, waits for them, and re-layouts: 11.4 us -> none  [pair_update(): outer_product.astype(jnp.bfloat16).reshape(n_rows * n_cols, -1)]
    reduce_sum x4 -> x0, other arithmetic: 9.75 us -> none  [the longest x2 5.17 us: standardize_embedding(): var = jnp.mean((x - mean) * (x - mean), axis=-1, keepdims=True)]
    unnamed x21, local copies, waits for them, and re-layouts: 12.3 us -> 5.63 us
    convert_element_type x2 -> x0, other arithmetic: 2.41 us -> none  [the longest x1 1.24 us: local(): return (tile + update).astype(jnp.bfloat16)]
  transfers between devices with their start and end apart: 1 -> 0, of which waited for: 1 -> 0; matrix products, arithmetic and copies ran while one was open for 3% -> 0% of each run, Pallas kernels for 0% -> 0%
where the time goes in v1:
time: 24.4 us; the launch traced here: 24.1 us
  Pallas kernels  18.4 us (75%)
  local copies, waits for them, and re-layouts  5.63 us (23%)
    pallas_call x1, Pallas kernels, local(): pl.pallas_call(functools.partial(kernel, n_row), out_shape=jax.ShapeDtype...  18.4 us
    unnamed x21, local copies, waits for them, and re-layouts  5.63 us

profile of v1, /device:TPU:1, one launch (start us, length us, event | category | flops | bytes accessed | tf_op | source)
XLA Modules:
  0.0 24.1 jit_solution(15642088018460542766)
XLA Ops:
  0.0 0.0 copy-start.8
  0.0 0.8 %copy.11.left_w_ref = bf16[256,32]{1,0:T(8,128)(2,1)S(1)} copy(bf16[256,32]{0,1:T(8,128)(2,1)} %param.13) | data formatting | bytes 32768 | tf_op args[3]
  0.9 0.0 copy-done.8
  0.9 0.0 copy-start.3
  0.9 0.0 copy-start.4
  0.9 0.0 copy-start.5
  0.9 0.0 copy-start.6
  0.9 0.0 copy-start.7
  0.9 0.1 copy.12.right_w_ref
  1.0 0.5 %copy-done.3 = f32[256]{0:T(256)S(1)} copy-done((f32[256]{0:T(256)S(1)}, f32[256]{0:T(256)}, u32[]{:S(2)}) %copy-start.3) | copy-done | bytes 1048
  1.5 0.0 copy-done.4
  1.6 0.0 copy-done.5
  1.6 0.0 copy-done.6
  1.6 0.0 copy-done.7
  1.6 0.0 copy-start
  1.6 1.2 %copy-done = bf16[16,256,128]{2,1,0:T(8,128)(2,1)S(1)} copy-done((bf16[16,256,128]{2,1,0:T(8,128)(2,1)S(1)}, bf16[16,256,128]{2,1,0:T(8,128)(2,1)}, u32[]{:S(2)}) %copy-start) | copy-done | bytes 1048600
  2.8 0.0 copy-start.1
  2.8 0.9 %copy-done.1 = bf16[32,16,256]{2,1,0:T(8,128)(2,1)S(1)} copy-done((bf16[32,16,256]{2,1,0:T(8,128)(2,1)S(1)}, bf16[32,16,256]{2,1,0:T(8,128)(2,1)}, u32[]{:S(2)}) %copy-start.1) | copy-done | bytes 262168
  3.8 0.0 copy-start.2
  3.8 0.9 %copy-done.2 = bf16[1024,128]{1,0:T(8,128)(2,1)S(1)} copy-done((bf16[1024,128]{1,0:T(8,128)(2,1)S(1)}, bf16[1024,128]{1,0:T(8,128)(2,1)}, u32[]{:S(2)}) %copy-start.2) | copy-done | bytes 262168
  4.7 18.4 %shard_map.100 = bf16[16,256,128]{2,1,0:T(8,128)(2,1)S(1)} custom-call(bf16[32,16,256]{2,1,0:T(8,128)(2,1)S(1)} %copy-done.1, f32[256]{0:T(256)S(1)} %copy-done.3, f32[256]{0:T(256)S(1)} %copy-done.4, bf16[256,32]{1,0:T(8,128)(2,1)S(1)} %copy.11.left_w_ref, f32[32]{0:T(128)S(1)} %copy-done.5, bf16[256,32]{1,0:T(8,128)(2,1)S(1)} %copy.12.right_w_ref, ...), custom_call_target="tpu_custom_call" | custom-call | tf_op jit(solution)/shard_map/pallas_call | solution.py:206
  23.1 1.0 %copy.14 = bf16[16,256,128]{2,1,0:T(8,128)(2,1)} copy(bf16[16,256,128]{2,1,0:T(8,128)(2,1)S(1)} %shard_map.100) | data formatting | bytes 2097152
Async XLA Ops:
  0.0 0.9 %copy-start.8 = (bf16[256,32]{0,1:T(8,128)(2,1)S(1)}, bf16[256,32]{0,1:T(8,128)(2,1)}, u32[]{:S(2)}) copy-start(bf16[256,32]{0,1:T(8,128)(2,1)} %param.15) | copy-start | bytes 49156
  0.9 0.7 %copy-start.3 = (f32[256]{0:T(256)S(1)}, f32[256]{0:T(256)}, u32[]{:S(2)}) copy-start(f32[256]{0:T(256)} %scale_ref.1) | copy-start | bytes 3076
  0.9 0.7 %copy-start.4 = (f32[256]{0:T(256)S(1)}, f32[256]{0:T(256)}, u32[]{:S(2)}) copy-start(f32[256]{0:T(256)} %shift_ref.1) | copy-start | bytes 3076
  0.9 0.7 %copy-start.5 = (f32[32]{0:T(128)S(1)}, f32[32]{0:T(128)}, u32[]{:S(2)}) copy-start(f32[32]{0:T(128)} %left_b_ref.1) | copy-start | bytes 388
  0.9 0.7 %copy-start.6 = (f32[32]{0:T(128)S(1)}, f32[32]{0:T(128)}, u32[]{:S(2)}) copy-start(f32[32]{0:T(128)} %right_b_ref.1) | copy-start | bytes 388
  0.9 0.7 %copy-start.7 = (f32[128]{0:T(128)S(1)}, f32[128]{0:T(128)}, u32[]{:S(2)}) copy-start(f32[128]{0:T(128)} %final_b_ref.1) | copy-start | bytes 1540
  1.6 1.2 %copy-start = (bf16[16,256,128]{2,1,0:T(8,128)(2,1)S(1)}, bf16[16,256,128]{2,1,0:T(8,128)(2,1)}, u32[]{:S(2)}) copy-start(bf16[16,256,128]{2,1,0:T(8,128)(2,1)} %pair_hbm.1) | copy-start | bytes 3145732
  2.8 0.9 %copy-start.1 = (bf16[32,16,256]{2,1,0:T(8,128)(2,1)S(1)}, bf16[32,16,256]{2,1,0:T(8,128)(2,1)}, u32[]{:S(2)}) copy-start(bf16[32,16,256]{2,1,0:T(8,128)(2,1)} %x_ref.1) | copy-start | bytes 786436
  3.8 0.9 %copy-start.2 = (bf16[1024,128]{1,0:T(8,128)(2,1)S(1)}, bf16[1024,128]{1,0:T(8,128)(2,1)}, u32[]{:S(2)}) copy-start(bf16[1024,128]{1,0:T(8,128)(2,1)} %final_hbm.1) | copy-start | bytes 786436

commit v2 on v1

--- a/solution.py
+++ b/solution.py
@@ -13,6 +13,17 @@
 
 def kernel(
     n_row,
+    x_hbm,
+    scale_hbm,
+    shift_hbm,
+    left_w_hbm,
+    left_b_hbm,
+    right_w_hbm,
+    right_b_hbm,
+    final_hbm,
+    final_b_hbm,
+    pair_hbm,
+    out_hbm,
     x_ref,
     scale_ref,
     shift_ref,
@@ -20,30 +31,46 @@
     left_b_ref,
     right_w_ref,
     right_b_ref,
-    final_hbm,
+    final_ref,
     final_b_ref,
-    pair_hbm,
-    out_hbm,
+    pair_ref,
     normed_ref,
-    final_ref,
     final32_ref,
     folded_ref,
     turned_ref,
     rows_ref,
     cols_ref,
-    pair_ref,
     out_ref,
-    pair_sem,
-    final_sem,
+    load_sem,
     out_sem,
     send_sem,
     recv_sem,
 ):
     depth, res, channels = x_ref.shape
-    width = left_w_ref.shape[1]
+    width = left_w_ref.shape[0]
     cz = final_b_ref.shape[0]
     pack = LANES // depth
     high = width // pack
+
+    loads = [
+        pltpu.make_async_copy(source, target, load_sem.at[index])
+        for index, (source, target) in enumerate(
+            (
+                (x_hbm, x_ref),
+                (scale_hbm, scale_ref),
+                (shift_hbm, shift_ref),
+                (right_w_hbm, right_w_ref),
+                (right_b_hbm, right_b_ref),
+                (left_w_hbm, left_w_ref),
+                (left_b_hbm, left_b_ref),
+                (final_hbm, final_ref),
+                (final_b_hbm, final_b_ref),
+                (pair_hbm, pair_ref),
+            )
+        )
+    ]
+    for copy in loads:
+        copy.start()
 
     me = lax.axis_index("row")
     core = lax.rem(me, 2)
@@ -54,20 +81,23 @@
     def place(z_, y_, core_):
         return z_ * 4 + y_ * 2 + core_
 
-    steps = sorted(range(1, nz), key=lambda d: (min(d, nz - d), d))
+    if nz == 4:
+        half = z // 2
+        near = 1 - (z + half * (3 - 2 * z))
+        others = [t + half * (3 - 2 * t) for t in (near, 2, 3)]
+    else:
+        steps = sorted(range(1, nz), key=lambda d: (min(d, nz - d), d))
+        others = [lax.rem(z + d, nz) for d in steps]
     across = place(z, 1 - y, core)
     sibling = place(z, y, 1 - core)
-    line = [place(lax.rem(z + d, nz), y, core) for d in steps]
+    line = [place(t, y, core) for t in others]
 
     barrier = pltpu.get_barrier_semaphore()
     for other in line + [across, sibling]:
         pl.semaphore_signal(barrier, inc=1, device_id={"row": other}, device_id_type=MESH)
 
-    pair_copy = pltpu.make_async_copy(pair_hbm, pair_ref, pair_sem)
-    final_copy = pltpu.make_async_copy(final_hbm, final_ref, final_sem)
-    final_copy.start()
-    pair_copy.start()
-
+    for copy in loads[:3]:
+        copy.wait()
     x = x_ref[...].astype(jnp.float32).reshape(depth * res, channels)
     mean = jnp.mean(x, axis=-1, keepdims=True)
     centred = x - mean
@@ -86,10 +116,12 @@
         axis=1,
     ).astype(jnp.bfloat16)
 
+    for copy in loads[3:5]:
+        copy.wait()
     right = lax.dot_general(
         right_w_ref[...],
         normed,
-        (((0,), (1,)), ((), ())),
+        (((1,), (1,)), ((), ())),
         preferred_element_type=jnp.float32,
     )
     right = right + right_b_ref[...][:, None]
@@ -142,9 +174,15 @@
     send(me, across)
     send(me, sibling)
 
-    left = jnp.dot(normed, left_w_ref[...], preferred_element_type=jnp.float32)
+    for copy in loads[5:8]:
+        copy.wait()
+    left = lax.dot_general(
+        normed,
+        left_w_ref[...],
+        (((1,), (1,)), ((), ())),
+        preferred_element_type=jnp.float32,
+    )
     left = (left + left_b_ref[...][None, :]).astype(jnp.bfloat16)
-    final_copy.wait()
     final32_ref[...] = final_ref[...].astype(jnp.float32)
 
     def fold(e):
@@ -161,22 +199,23 @@
 
     for e in range(0, width // 2, 2):
         fold(e)
-    for d in steps:
-        slot = place(lax.rem(z + nz - d, nz), y, core)
+    for t in others:
+        slot = place(t, y, core)
         arrived(slot)
         send(slot, across)
         send(slot, sibling)
     for e in range(width // 2, width, 2):
         fold(e)
-    for d in [0] + steps:
-        slot = place(lax.rem(z + nz - d, nz), 1 - y, core)
+    for t in [z] + others:
+        slot = place(t, 1 - y, core)
         arrived(slot)
         send(slot, sibling)
     for y_ in range(2):
-        for d in [0] + steps:
-            arrived(place(lax.rem(z + nz - d, nz), y_, 1 - core))
-
-    pair_copy.wait()
+        for t in [z] + others:
+            arrived(place(t, y_, 1 - core))
+
+    for copy in loads[8:]:
+        copy.wait()
     cols = cols_ref[...].reshape(n_row * res, width * depth)
     outs = []
     for i in range(0, res, 2):
@@ -201,33 +240,31 @@
     depth, res, channels = x.shape
     width = left_w.shape[1]
     cz = final_w.shape[1]
-    vmem = pl.BlockSpec(memory_space=pltpu.VMEM)
-    hbm = pl.BlockSpec(memory_space=pl.ANY)
+    hbm = pl.BlockSpec(memory_space=pltpu.HBM)
+    args = (x, scale, shift, left_w.T, left_b, right_w.T, right_b, final_w, final_b, pair)
     return pl.pallas_call(
         functools.partial(kernel, n_row),
         out_shape=jax.ShapeDtypeStruct(pair.shape, pair.dtype),
-        in_specs=[vmem] * 7 + [hbm, vmem, hbm],
+        in_specs=[hbm] * len(args),
         out_specs=hbm,
-        scratch_shapes=[
+        scratch_shapes=[pltpu.VMEM(arg.shape, arg.dtype) for arg in args]
+        + [
             pltpu.VMEM((channels // LANES, depth * res, LANES), jnp.float32),
-            pltpu.VMEM(final_w.shape, jnp.bfloat16),
             pltpu.VMEM(final_w.shape, jnp.float32),
             pltpu.VMEM((width * depth, res * cz), jnp.bfloat16),
             pltpu.VMEM((res * depth // LANES, width, LANES), jnp.float32),
             pltpu.VMEM((res * width * depth // LANES, LANES), jnp.float32),
             pltpu.VMEM((n_row, res, width * depth), jnp.bfloat16),
             pltpu.VMEM(pair.shape, jnp.bfloat16),
-            pltpu.VMEM(pair.shape, jnp.bfloat16),
-            pltpu.SemaphoreType.DMA,
-            pltpu.SemaphoreType.DMA,
+            pltpu.SemaphoreType.DMA((len(args),)),
             pltpu.SemaphoreType.DMA((res // 2,)),
             pltpu.SemaphoreType.DMA((n_row - 1,)),
             pltpu.SemaphoreType.DMA((n_row,)),
         ],
         compiler_params=pltpu.CompilerParams(
-            collective_id=0, has_side_effects=True, vmem_limit_bytes=48 * 1024 * 1024
+            collective_id=0, has_side_effects=True, vmem_limit_bytes=63 * 1024 * 1024
         ),
-    )(x, scale, shift, left_w, left_b, right_w, right_b, final_w, final_b, pair)
+    )(*args)
 
 
 def solution(mesh):

time: 24.4 us -> 18.7 us (0.77)
  local copies, waits for them, and re-layouts: 5.63 us -> 2.3 us
  Pallas kernels: 18.4 us -> 16.2 us
    unnamed x21 -> x1, local copies, waits for them, and re-layouts: 5.63 us -> 2.3 us
    pallas_call x1, Pallas kernels: 18.4 us -> 16.2 us  [local(): pl.pallas_call(functools.partial(kernel, n_row), out_shape=jax.ShapeDtype...]
where the time goes in v2:
time: 18.7 us; the launch traced here: 18.5 us
  Pallas kernels  16.2 us (87%)
  local copies, waits for them, and re-layouts  2.3 us (12%)
    pallas_call x1, Pallas kernels, local(): pl.pallas_call(functools.partial(kernel, n_row), out_shape=jax.ShapeDtype...  16.2 us
    unnamed x1, local copies, waits for them, and re-layouts  2.3 us

profile of v2, /device:TPU:1, one launch (start us, length us, event | category | flops | bytes accessed | tf_op | source)
XLA Modules:
  0.0 18.5 jit_solution(14598827107085146608)
XLA Ops:
  0.0 16.2 %shard_map.100 = bf16[16,256,128]{2,1,0:T(8,128)(2,1)} custom-call(bf16[32,16,256]{2,1,0:T(8,128)(2,1)} %x_hbm.1, f32[256]{0:T(256)} %scale_hbm.1, f32[256]{0:T(256)} %shift_hbm.1, bf16[32,256]{1,0:T(8,128)(2,1)} %bitcast.2, f32[32]{0:T(128)} %left_b_hbm.1, bf16[32,256]{1,0:T(8,128)(2,1)} %bitcast.3, f32[32]{0:T(128)} %right_b_hbm.1, ...), custom_call_target="tpu_custom_call" | custom-call | tf_op jit(solution)/shard_map/pallas_call | solution.py:245
  16.2 2.3 %copy.12 = bf16[16,256,128]{2,1,0:T(8,128)(2,1)} copy(bf16[16,256,128]{2,1,0:T(8,128)(2,1)} %shard_map.100) | data formatting | bytes 2097152

commit v3 on v2

--- a/solution.py
+++ b/solution.py
@@ -23,7 +23,7 @@
     final_hbm,
     final_b_hbm,
     pair_hbm,
-    out_hbm,
+    out_ref,
     x_ref,
     scale_ref,
     shift_ref,
@@ -40,9 +40,7 @@
     turned_ref,
     rows_ref,
     cols_ref,
-    out_ref,
     load_sem,
-    out_sem,
     send_sem,
     recv_sem,
 ):
@@ -69,7 +67,7 @@
             )
         )
     ]
-    for copy in loads:
+    for copy in loads[:5]:
         copy.start()
 
     me = lax.axis_index("row")
@@ -144,6 +142,8 @@
         [rows_ref[pl.ds(h, res, stride=high), :] for h in range(high)], axis=1
     ).astype(jnp.bfloat16)
 
+    for copy in loads[5:]:
+        copy.start()
     pl.semaphore_wait(barrier, nz + 1)
     sends = []
 
@@ -217,7 +217,6 @@
     for copy in loads[8:]:
         copy.wait()
     cols = cols_ref[...].reshape(n_row * res, width * depth)
-    outs = []
     for i in range(0, res, 2):
         update = jnp.dot(
             cols, folded_ref[:, i * cz : (i + 2) * cz], preferred_element_type=jnp.float32
@@ -225,28 +224,23 @@
         for k in range(2):
             part = update[:, k * cz : (k + 1) * cz] + final_b_ref[...][None, :]
             out_ref[i + k] = (pair_ref[i + k].astype(jnp.float32) + part).astype(jnp.bfloat16)
-        copy = pltpu.make_async_copy(
-            out_ref.at[pl.ds(i, 2)], out_hbm.at[pl.ds(i, 2)], out_sem.at[i // 2]
-        )
-        copy.start()
-        outs.append(copy)
     for copy in sends:
         copy.wait_send()
-    for copy in outs:
-        copy.wait()
 
 
 def local(n_row, x, scale, shift, left_w, left_b, right_w, right_b, final_w, final_b, pair):
     depth, res, channels = x.shape
     width = left_w.shape[1]
     cz = final_w.shape[1]
+    vmem = pl.BlockSpec(memory_space=pltpu.VMEM)
     hbm = pl.BlockSpec(memory_space=pltpu.HBM)
     args = (x, scale, shift, left_w.T, left_b, right_w.T, right_b, final_w, final_b, pair)
+    args = tuple(pltpu.with_memory_space_constraint(arg, pltpu.HBM) for arg in args)
     return pl.pallas_call(
         functools.partial(kernel, n_row),
         out_shape=jax.ShapeDtypeStruct(pair.shape, pair.dtype),
         in_specs=[hbm] * len(args),
-        out_specs=hbm,
+        out_specs=vmem,
         scratch_shapes=[pltpu.VMEM(arg.shape, arg.dtype) for arg in args]
         + [
             pltpu.VMEM((channels // LANES, depth * res, LANES), jnp.float32),
@@ -255,14 +249,12 @@
             pltpu.VMEM((res * depth // LANES, width, LANES), jnp.float32),
             pltpu.VMEM((res * width * depth // LANES, LANES), jnp.float32),
             pltpu.VMEM((n_row, res, width * depth), jnp.bfloat16),
-            pltpu.VMEM(pair.shape, jnp.bfloat16),
             pltpu.SemaphoreType.DMA((len(args),)),
-            pltpu.SemaphoreType.DMA((res // 2,)),
             pltpu.SemaphoreType.DMA((n_row - 1,)),
             pltpu.SemaphoreType.DMA((n_row,)),
         ],
         compiler_params=pltpu.CompilerParams(
-            collective_id=0, has_side_effects=True, vmem_limit_bytes=63 * 1024 * 1024
+            collective_id=0, has_side_effects=True, vmem_limit_bytes=48 * 1024 * 1024
         ),
     )(*args)
 

time: 18.7 us -> 16.6 us (0.89)
  local copies, waits for them, and re-layouts: 2.3 us -> 0.97 us
  Pallas kernels: 16.2 us -> 15.5 us
    unnamed x1, local copies, waits for them, and re-layouts: 2.3 us -> 0.97 us
    pallas_call x1, Pallas kernels: 16.2 us -> 15.5 us  [local(): pl.pallas_call(functools.partial(kernel, n_row), out_shape=jax.ShapeDtype...]
where the time goes in v3:
time: 16.6 us; the launch traced here: 16.4 us
  Pallas kernels  15.5 us (93%)
  local copies, waits for them, and re-layouts  0.97 us (6%)
    pallas_call x1, Pallas kernels, local(): pl.pallas_call(functools.partial(kernel, n_row), out_shape=jax.ShapeDtype...  15.5 us
    unnamed x1, local copies, waits for them, and re-layouts  0.97 us

profile of v3, /device:TPU:1, one launch (start us, length us, event | category | flops | bytes accessed | tf_op | source)
XLA Modules:
  0.0 16.4 jit_solution(7073934527383752922)
XLA Ops:
  0.0 15.5 %shard_map.100 = bf16[16,256,128]{2,1,0:T(8,128)(2,1)S(1)} custom-call(bf16[32,16,256]{2,1,0:T(8,128)(2,1)} %x_hbm.1, f32[256]{0:T(256)} %scale_hbm.1, f32[256]{0:T(256)} %shift_hbm.1, bf16[32,256]{1,0:T(8,128)(2,1)} %bitcast.2, f32[32]{0:T(128)} %left_b_hbm.1, bf16[32,256]{1,0:T(8,128)(2,1)} %bitcast.3, f32[32]{0:T(128)} %right_b_hbm.1, ...), custom_call_target="tpu_custom_call" | custom-call | tf_op jit(solution)/shard_map/pallas_call | solution.py:239
  15.5 1.0 %copy.12 = bf16[16,256,128]{2,1,0:T(8,128)(2,1)} copy(bf16[16,256,128]{2,1,0:T(8,128)(2,1)S(1)} %shard_map.100) | data formatting | bytes 2097152

commit v4 on v3

--- a/solution.py
+++ b/solution.py
@@ -88,10 +88,11 @@
         others = [lax.rem(z + d, nz) for d in steps]
     across = place(z, 1 - y, core)
     sibling = place(z, y, 1 - core)
+    corner = place(z, 1 - y, 1 - core)
     line = [place(t, y, core) for t in others]
 
     barrier = pltpu.get_barrier_semaphore()
-    for other in line + [across, sibling]:
+    for other in line + [across, corner, sibling]:
         pl.semaphore_signal(barrier, inc=1, device_id={"row": other}, device_id_type=MESH)
 
     for copy in loads[:3]:
@@ -144,7 +145,7 @@
 
     for copy in loads[5:]:
         copy.start()
-    pl.semaphore_wait(barrier, nz + 1)
+    pl.semaphore_wait(barrier, nz + 2)
     sends = []
 
     def send(slot, target):
@@ -171,8 +172,8 @@
 
     for target in line:
         send(me, target)
-    send(me, across)
-    send(me, sibling)
+    for target in (across, corner, sibling):
+        send(me, target)
 
     for copy in loads[5:8]:
         copy.wait()
@@ -202,17 +203,13 @@
     for t in others:
         slot = place(t, y, core)
         arrived(slot)
-        send(slot, across)
-        send(slot, sibling)
+        for target in (across, corner, sibling):
+            send(slot, target)
     for e in range(width // 2, width, 2):
         fold(e)
-    for t in [z] + others:
-        slot = place(t, 1 - y, core)
-        arrived(slot)
-        send(slot, sibling)
-    for y_ in range(2):
+    for y_, core_ in ((y, 1 - core), (1 - y, core), (1 - y, 1 - core)):
         for t in [z] + others:
-            arrived(place(t, y_, 1 - core))
+            arrived(place(t, y_, core_))
 
     for copy in loads[8:]:
         copy.wait()

time: 16.6 us -> 15.9 us (0.958)
  the two profiles are of different devices: /device:TPU:1 before, /device:TPU:0 now
where the time goes in v4:
time: 15.9 us; the launch traced here: 15.7 us
  Pallas kernels  14.8 us (93%)
  local copies, waits for them, and re-layouts  0.97 us (6%)
    pallas_call x1, Pallas kernels, local(): pl.pallas_call(functools.partial(kernel, n_row), out_shape=jax.ShapeDtype...  14.8 us
    unnamed x1, local copies, waits for them, and re-layouts  0.97 us

profile of v4, /device:TPU:0, one launch (start us, length us, event | category | flops | bytes accessed | tf_op | source)
XLA Modules:
  0.0 15.7 jit_solution(5422244847991253676)
XLA Ops:
  0.0 14.8 %shard_map.100 = bf16[16,256,128]{2,1,0:T(8,128)(2,1)S(1)} custom-call(bf16[32,16,256]{2,1,0:T(8,128)(2,1)} %x_hbm.1, f32[256]{0:T(256)} %scale_hbm.1, f32[256]{0:T(256)} %shift_hbm.1, bf16[32,256]{1,0:T(8,128)(2,1)} %bitcast.2, f32[32]{0:T(128)} %left_b_hbm.1, bf16[32,256]{1,0:T(8,128)(2,1)} %bitcast.3, f32[32]{0:T(128)} %right_b_hbm.1, ...), custom_call_target="tpu_custom_call" | custom-call | tf_op jit(solution)/shard_map/pallas_call | solution.py:236
  14.8 1.0 %copy.12 = bf16[16,256,128]{2,1,0:T(8,128)(2,1)} copy(bf16[16,256,128]{2,1,0:T(8,128)(2,1)S(1)} %shard_map.100) | data formatting | bytes 2097152

commit v5 on v4

--- a/solution.py
+++ b/solution.py
@@ -198,14 +198,12 @@
                     i * depth : (i + 1) * depth, k * cz : (k + 1) * cz
                 ]
 
-    for e in range(0, width // 2, 2):
-        fold(e)
     for t in others:
         slot = place(t, y, core)
         arrived(slot)
         for target in (across, corner, sibling):
             send(slot, target)
-    for e in range(width // 2, width, 2):
+    for e in range(0, width, 2):
         fold(e)
     for y_, core_ in ((y, 1 - core), (1 - y, core), (1 - y, 1 - core)):
         for t in [z] + others:

time: 15.9 us -> 15.9 us (level)
  no operation moved by 1% of the time
where the time goes in v5:
time: 15.9 us; the launch traced here: 15.7 us
  Pallas kernels  14.8 us (93%)
  local copies, waits for them, and re-layouts  0.97 us (6%)
    pallas_call x1, Pallas kernels, local(): pl.pallas_call(functools.partial(kernel, n_row), out_shape=jax.ShapeDtype...  14.8 us
    unnamed x1, local copies, waits for them, and re-layouts  0.97 us

profile of v5, /device:TPU:0, one launch (start us, length us, event | category | flops | bytes accessed | tf_op | source)
XLA Modules:
  0.0 15.7 jit_solution(517818502712745862)
XLA Ops:
  0.0 14.8 %shard_map.100 = bf16[16,256,128]{2,1,0:T(8,128)(2,1)S(1)} custom-call(bf16[32,16,256]{2,1,0:T(8,128)(2,1)} %x_hbm.1, f32[256]{0:T(256)} %scale_hbm.1, f32[256]{0:T(256)} %shift_hbm.1, bf16[32,256]{1,0:T(8,128)(2,1)} %bitcast.2, f32[32]{0:T(128)} %left_b_hbm.1, bf16[32,256]{1,0:T(8,128)(2,1)} %bitcast.3, f32[32]{0:T(128)} %right_b_hbm.1, ...), custom_call_target="tpu_custom_call" | custom-call | tf_op jit(solution)/shard_map/pallas_call | solution.py:234
  14.8 1.0 %copy.12 = bf16[16,256,128]{2,1,0:T(8,128)(2,1)} copy(bf16[16,256,128]{2,1,0:T(8,128)(2,1)S(1)} %shard_map.100) | data formatting | bytes 2097152
